TPU v7x, 32 devices: a whole 2x2x4 slice. The times are simulated.
32 devices in a mesh: req: 4 (over y, x), tp: 8 (over z, core).
Axes of the slice: x: 2, y: 2, z: 4, core: 2. Of those that a mesh axis runs over, the one named last changes fastest.
Arguments:
- step_inputs: bfloat16 [4, 256, 1536], P(None, ('req', 'tp')), may hold values from -6 to 6
- qkv_weight: bfloat16 [1536, 2048], replicated, may hold values from -0.15625 to 0.15625
- qkv_bias: float32 [2048], replicated, may hold values from -8 to 8
- out_weight: bfloat16 [1536, 1536], P('tp'), may hold values from -0.15625 to 0.15625
- gate_weight: bfloat16 [1536, 8960], P(None, 'tp'), may hold values from -0.15625 to 0.15625
- up_weight: bfloat16 [1536, 8960], P(None, 'tp'), may hold values from -0.15625 to 0.15625
- down_weight: bfloat16 [8960, 1536], P('tp'), may hold values from -0.0625 to 0.0625
- cache_keys: bfloat16 [256, 4096, 256], P(('req', 'tp')), may hold values from -60 to 60
- cache_values: bfloat16 [256, 4096, 256], P(('req', 'tp')), may hold values from -24 to 24
- lengths: int32 [32, 8], replicated, may hold values from 1 to 4096, as said below
- parents: int32 [4, 32, 8], replicated, may hold values from 0 to 7
- slot_request: int32 [32], replicated, may hold values from 0 to 31, each once
Outputs:
- outputs: bfloat16 [4, 256, 1536], P(None, ('req', 'tp'))
Inputs may be any that keep to these rules, and one draw needn't show every extreme that they name: lengths[r, c] is the number of cached positions of beam c of request r; some beam has exactly 4096. parents[t, r, b] names a beam of the same request r. `slot_request`: a permutation of the requests; slots 8 * i to 8 * i + 7 are rows of index i of req.
All inputs are finite; a program needn't handle non-finite values.
Results may differ from a plain program's by a relative error of at most 0.022.
The roundings to bfloat16 on the way count: a program that leaves them out, or rounds other values in their place, can miss the bound.
Values may be sent and summed in bfloat16 or wider, within the bound.
A program may use at most 192 MiB of HBM per device.

v0:
```python
import functools

import jax
import jax.numpy as jnp
from jax import lax
from jax.experimental import pallas as pl
from jax.experimental.pallas import tpu as pltpu
from jax.sharding import PartitionSpec as P

Q_HEADS = 12
KV_HEADS = 2


theta_base = 1000000.0
norm_eps = 1e-06
masked_score = -1e30


def rms_normed(values):
    values = values.astype(jnp.float32)
    factor = lax.rsqrt(jnp.mean(values * values, axis=-1, keepdims=True) + norm_eps)
    return (values * factor).astype(jnp.bfloat16)


def rotate(vectors, positions):
    half = vectors.shape[-1] // 2
    freqs = theta_base ** (-jnp.arange(half, dtype=jnp.float32) * 2.0 / vectors.shape[-1])
    angles = positions.astype(jnp.float32)[:, None] * freqs[None, :]
    cosine = jnp.cos(angles)[:, None, :]
    sine = jnp.sin(angles)[:, None, :]
    values = vectors.astype(jnp.float32)
    first = values[..., :half]
    second = values[..., half:]
    return jnp.concatenate(
        [first * cosine - second * sine, second * cosine + first * sine], axis=-1
    ).astype(jnp.bfloat16)


def owner_rows(flat, owned_count, beams, inverse):
    owned_global = flat * owned_count + jnp.arange(owned_count, dtype=jnp.int32)
    owned_request = owned_global // beams
    owned_beam = owned_global % beams
    beam_range = jnp.arange(beams, dtype=jnp.int32)
    query_rows = (inverse[owned_request][:, None] * beams + beam_range[None, :]).reshape(-1)
    return (owned_request, owned_beam, query_rows)


def owned_attention(
    every_query, keys, values, owned_request, owned_beam, query_rows, root_all, lengths
):
    owned_rows, context, kv_width = keys.shape
    beams = root_all.shape[1]
    head_dim = kv_width // KV_HEADS
    group = Q_HEADS // KV_HEADS
    grouped = jnp.take(every_query, query_rows, axis=0).reshape(
        owned_rows, beams, KV_HEADS, group, head_dim
    )
    keys = keys.reshape(owned_rows, context, KV_HEADS, head_dim)
    values = values.reshape(owned_rows, context, KV_HEADS, head_dim)
    scores = jnp.einsum(
        "jbkgd,jpkd->jbkgp", grouped, keys, preferred_element_type=jnp.float32
    ) * head_dim ** (-0.5)
    limits = lengths[owned_request, owned_beam]
    live = (jnp.arange(context, dtype=jnp.int32)[None, :] < limits[:, None])[:, None, None, None, :]
    scores = jnp.where(live, scores, masked_score)
    peak = jnp.max(scores, axis=-1)
    weights = jnp.where(live, jnp.exp(scores - peak[..., None]), 0.0)
    total = jnp.sum(weights, axis=-1)
    output = jnp.einsum(
        "jbkgp,jpkd->jbkgd",
        weights.astype(jnp.bfloat16),
        values,
        preferred_element_type=jnp.float32,
    )
    chosen = (root_all[owned_request] == owned_beam[:, None])[:, :, None, None]
    peak = jnp.where(chosen, peak, 0.0).reshape(owned_rows * beams, KV_HEADS, group)
    total = jnp.where(chosen, total, 0.0).reshape(owned_rows * beams, KV_HEADS, group)
    output = jnp.where(chosen[..., None], output, 0.0).reshape(
        owned_rows * beams, KV_HEADS, group, head_dim
    )
    return (peak, total, output)


def spread_rows(pieces, target_rows, row_count):
    return tuple(
        (
            jnp.zeros((row_count,) + piece.shape[1:], jnp.float32).at[target_rows].add(piece)
            for piece in pieces
        )
    )


def per_device_split(
    step_inputs,
    qkv_weight,
    qkv_bias,
    out_weight,
    gate_weight,
    up_weight,
    down_weight,
    cache_keys,
    cache_values,
    lengths,
    parents,
    slot_request,
):
    steps_count, rows_dev, width = step_inputs.shape
    beams = parents.shape[2]
    requests = slot_request.shape[0]
    req_count = lax.axis_size("req")
    tp_count = lax.axis_size("tp")
    group_requests = requests // req_count
    group_rows = group_requests * beams
    total_rows = requests * beams
    owned_count = cache_keys.shape[0]
    kv_width = cache_keys.shape[2]
    head_dim = kv_width // KV_HEADS
    group = Q_HEADS // KV_HEADS
    attn_width = Q_HEADS * head_dim
    req_index = lax.axis_index("req")
    tp_index = lax.axis_index("tp")
    flat_index = req_index * tp_count + tp_index
    my_requests = lax.dynamic_slice_in_dim(slot_request, req_index * group_requests, group_requests)
    inverse = (
        jnp.zeros((requests,), jnp.int32)
        .at[slot_request]
        .set(jnp.arange(requests, dtype=jnp.int32))
    )
    owned_request, owned_beam, query_rows = owner_rows(flat_index, owned_count, beams, inverse)
    beam_range = jnp.arange(beams, dtype=jnp.int32)
    root_all = jnp.broadcast_to(beam_range[None, :], (requests, beams))
    gen_keys = jnp.zeros((steps_count, group_rows, kv_width), jnp.bfloat16)
    gen_values = jnp.zeros((steps_count, group_rows, kv_width), jnp.bfloat16)
    base_rows = (jnp.arange(group_requests, dtype=jnp.int32) * beams)[:, None]
    column_width = out_weight.shape[0]
    results = []
    for step in range(steps_count):
        root_all = jnp.take_along_axis(root_all, parents[step], axis=1)
        reorder = (base_rows + parents[step][my_requests]).reshape(-1)
        gen_keys = jnp.take(gen_keys, reorder, axis=1)
        gen_values = jnp.take(gen_values, reorder, axis=1)
        inputs = step_inputs[step]
        normed = rms_normed(inputs)
        qkv = (
            jnp.dot(
                lax.all_gather(normed, "tp", axis=0, tiled=True),
                qkv_weight,
                preferred_element_type=jnp.float32,
            )
            + qkv_bias
        ).astype(jnp.bfloat16)
        my_roots = root_all[my_requests]
        positions = (jnp.take_along_axis(lengths[my_requests], my_roots, axis=1) + step).reshape(-1)
        queries = rotate(qkv[:, :attn_width].reshape(group_rows, Q_HEADS, head_dim), positions)
        new_keys = rotate(
            qkv[:, attn_width : attn_width + kv_width].reshape(group_rows, KV_HEADS, head_dim),
            positions,
        )
        gen_keys = gen_keys.at[step].set(new_keys.reshape(group_rows, kv_width))
        gen_values = gen_values.at[step].set(qkv[:, attn_width + kv_width :])
        every_query = lax.all_gather(
            queries.reshape(group_rows, attn_width), "req", axis=0, tiled=True
        )
        part_peak, part_total, part_output = owned_attention(
            every_query,
            cache_keys,
            cache_values,
            owned_request,
            owned_beam,
            query_rows,
            root_all,
            lengths,
        )
        all_peak, all_total, all_output = spread_rows(
            (part_peak, part_total, part_output), query_rows, total_rows
        )
        sum_peak, sum_total, sum_output = lax.psum((all_peak, all_total, all_output), ("req", "tp"))
        peak = lax.dynamic_slice_in_dim(sum_peak, req_index * group_rows, group_rows, 0)
        total = lax.dynamic_slice_in_dim(sum_total, req_index * group_rows, group_rows, 0)
        output = lax.dynamic_slice_in_dim(sum_output, req_index * group_rows, group_rows, 0)
        grouped = queries.reshape(group_rows, KV_HEADS, group, head_dim)
        past_keys = gen_keys[: step + 1].reshape(step + 1, group_rows, KV_HEADS, head_dim)
        past_values = gen_values[: step + 1].reshape(step + 1, group_rows, KV_HEADS, head_dim)
        recent_scores = jnp.einsum(
            "bkgd,sbkd->bkgs", grouped, past_keys, preferred_element_type=jnp.float32
        ) * head_dim ** (-0.5)
        top = jnp.maximum(peak, jnp.max(recent_scores, axis=-1))
        factor = jnp.exp(peak - top)
        recent_weights = jnp.exp(recent_scores - top[..., None])
        denominator = total * factor + jnp.sum(recent_weights, axis=-1)
        numerator = output * factor[..., None] + jnp.einsum(
            "bkgs,sbkd->bkgd",
            recent_weights.astype(jnp.bfloat16),
            past_values,
            preferred_element_type=jnp.float32,
        )
        attention = (
            (numerator / denominator[..., None])
            .reshape(group_rows, attn_width)
            .astype(jnp.bfloat16)
        )
        columns = lax.dynamic_slice_in_dim(attention, tp_index * column_width, column_width, 1)
        attended = lax.psum_scatter(
            jnp.dot(columns, out_weight, preferred_element_type=jnp.float32).astype(jnp.bfloat16),
            "tp",
            scatter_dimension=0,
            tiled=True,
        ).astype(jnp.float32)
        middle = inputs.astype(jnp.float32) + attended
        mixed_in = rms_normed(middle)
        piece = lax.all_gather(mixed_in, "tp", axis=0, tiled=True)
        gate = jnp.dot(piece, gate_weight, preferred_element_type=jnp.float32)
        upward = jnp.dot(piece, up_weight, preferred_element_type=jnp.float32)
        hidden = (jax.nn.silu(gate) * upward).astype(jnp.bfloat16)
        lowered = lax.psum_scatter(
            jnp.dot(hidden, down_weight, preferred_element_type=jnp.float32).astype(jnp.bfloat16),
            "tp",
            scatter_dimension=0,
            tiled=True,
        ).astype(jnp.float32)
        results.append((middle + lowered).astype(jnp.bfloat16))
    return jnp.stack(results)

MESH = pl.DeviceIdType.MESH
CHUNK = 4
KEY_BLOCK = 2048
HEAD_ROWS = 16


def greet(axes):
    barrier = pltpu.get_barrier_semaphore()
    total = 0
    for axis, count in axes:
        me = lax.axis_index(axis)
        for hop in range(1, count):
            peer = lax.rem(me + hop, count)
            pl.semaphore_signal(barrier, inc=1, device_id={axis: peer}, device_id_type=MESH)
        total += count - 1
    pl.semaphore_wait(barrier, total)


def start_exchange(axis, count, source, target, send_sem, recv_sem):
    me = lax.axis_index(axis)
    copies = []
    for hop in range(1, count):
        peer = lax.rem(me + hop, count)
        copy = pltpu.make_async_remote_copy(
            src_ref=source(peer),
            dst_ref=target(me),
            send_sem=send_sem.at[hop - 1],
            recv_sem=recv_sem.at[hop - 1],
            device_id={axis: peer},
            device_id_type=MESH,
        )
        copy.start()
        copies.append(copy)
    return copies


def wait_all(copies):
    for copy in copies:
        copy.wait()


def route_kernel(
    req_count, tp_count, pick_ref, x_ref, o_ref, first, second, staged, sends, recvs
):
    req_me = lax.axis_index("req")
    tp_me = lax.axis_index("tp")
    piece = x_ref.shape[1] // tp_count
    greet((("tp", tp_count), ("req", req_count)))

    def columns(peer):
        return x_ref.at[:, pl.ds(pl.multiple_of(peer * piece, piece), piece)]

    copies = start_exchange(
        "tp", tp_count, columns, lambda me: first.at[me], sends.at[0], recvs.at[0]
    )
    first[tp_me] = x_ref[:, pl.ds(pl.multiple_of(tp_me * piece, piece), piece)]
    wait_all(copies)
    group = pl.ds(req_me * tp_count, tp_count)
    copies = start_exchange(
        "req", req_count, lambda peer: first, lambda me: second.at[group], sends.at[1], recvs.at[1]
    )
    second[group] = first[...]
    wait_all(copies)
    for target in range(tp_count):
        staged[target] = second[pick_ref[target]]
    copies = start_exchange(
        "tp",
        tp_count,
        lambda peer: staged.at[peer],
        lambda me: o_ref.at[me],
        sends.at[2],
        recvs.at[2],
    )
    o_ref[tp_me] = staged[tp_me]
    wait_all(copies)


def route(x, pick, req_count, tp_count):
    rows, width = x.shape
    piece = width // tp_count
    most = max(req_count, tp_count)
    return pl.pallas_call(
        functools.partial(route_kernel, req_count, tp_count),
        out_shape=jax.ShapeDtypeStruct((tp_count, rows, piece), x.dtype),
        in_specs=[
            pl.BlockSpec(memory_space=pltpu.SMEM),
            pl.BlockSpec(memory_space=pltpu.VMEM),
        ],
        out_specs=pl.BlockSpec(memory_space=pltpu.VMEM),
        scratch_shapes=[
            pltpu.VMEM((tp_count, rows, piece), x.dtype),
            pltpu.VMEM((req_count * tp_count, rows, piece), x.dtype),
            pltpu.VMEM((tp_count, rows, piece), x.dtype),
            pltpu.SemaphoreType.DMA((3, most)),
            pltpu.SemaphoreType.DMA((3, most)),
        ],
        compiler_params=pltpu.CompilerParams(
            collective_id=0, has_side_effects=True, vmem_limit_bytes=32 * 1024 * 1024
        ),
        name="route",
    )(pick, x)


def attention_kernel(
    pairs,
    order_ref,
    begin_ref,
    count_ref,
    limit_ref,
    beam_ref,
    block_ref,
    total_ref,
    q_ref,
    kn_ref,
    vn_ref,
    seen_ref,
    k_ref,
    v_ref,
    o_ref,
    qs,
    top_s,
    sum_s,
    acc_s,
):
    item = pl.program_id(0)
    head_dim = o_ref.shape[-1]
    width = q_ref.shape[-1]
    scale = head_dim ** (-0.5)
    contract = (((1,), (1,)), ((), ()))
    key_block = k_ref.shape[0]

    @pl.when(item == 0)
    def _():
        for place in range(pairs):
            qs[place] = q_ref[order_ref[place]]
        qs[pairs:] = jnp.zeros((CHUNK,) + qs.shape[1:], qs.dtype)
        rows = pairs * HEAD_ROWS
        scores = scale * lax.dot_general(
            qs[:pairs].reshape(rows, width),
            kn_ref[...],
            contract,
            preferred_element_type=jnp.float32,
        )
        seen = seen_ref[...] > 0.5
        scores = jnp.where(seen, scores, masked_score)
        top = jnp.max(scores, axis=1, keepdims=True)
        weights = jnp.where(seen, jnp.exp(scores - top), 0.0)
        total = jnp.sum(weights, axis=1, keepdims=True)
        mixed = jnp.dot(
            weights.astype(jnp.bfloat16), vn_ref[...], preferred_element_type=jnp.float32
        )
        top_s[:pairs] = jnp.broadcast_to(top, (rows, 128)).reshape(pairs, HEAD_ROWS, 128)
        sum_s[:pairs] = jnp.broadcast_to(total, (rows, 128)).reshape(pairs, HEAD_ROWS, 128)
        acc_s[:pairs] = mixed.reshape(pairs, HEAD_ROWS, width)
        top_s[pairs:] = jnp.zeros((CHUNK, HEAD_ROWS, 128), jnp.float32)
        sum_s[pairs:] = jnp.zeros((CHUNK, HEAD_ROWS, 128), jnp.float32)
        acc_s[pairs:] = jnp.zeros((CHUNK, HEAD_ROWS, width), jnp.float32)

    @pl.when(item < total_ref[0])
    def _():
        beam = beam_ref[item]
        begin = begin_ref[beam]
        end = begin + count_ref[beam]
        left = limit_ref[beam] - block_ref[item] * key_block
        rows = CHUNK * HEAD_ROWS

        def one_chunk(index, carry):
            base = begin + index * CHUNK
            span = pl.ds(base, CHUNK)
            scores = scale * lax.dot_general(
                qs[span].reshape(rows, width),
                k_ref[...],
                contract,
                preferred_element_type=jnp.float32,
            )
            place = lax.broadcasted_iota(jnp.int32, (rows, key_block), 1)
            row = lax.broadcasted_iota(jnp.int32, (rows, 1), 0)
            live = place < jnp.where(row < (end - base) * HEAD_ROWS, left, 0)
            scores = jnp.where(live, scores, masked_score)
            old = top_s[span].reshape(rows, 128)[:, :1]
            top = jnp.maximum(old, jnp.max(scores, axis=1, keepdims=True))
            weights = jnp.exp(scores - top)
            fade = jnp.exp(old - top)
            total = sum_s[span].reshape(rows, 128)[:, :1] * fade
            total = total + jnp.sum(weights, axis=1, keepdims=True)
            mixed = acc_s[span].reshape(rows, width) * fade + jnp.dot(
                weights.astype(jnp.bfloat16), v_ref[...], preferred_element_type=jnp.float32
            )
            top_s[span] = jnp.broadcast_to(top, (rows, 128)).reshape(CHUNK, HEAD_ROWS, 128)
            sum_s[span] = jnp.broadcast_to(total, (rows, 128)).reshape(CHUNK, HEAD_ROWS, 128)
            acc_s[span] = mixed.reshape(CHUNK, HEAD_ROWS, width)
            return carry

        lax.fori_loop(0, lax.div(end - begin + CHUNK - 1, CHUNK), one_chunk, 0)

    @pl.when(item == pl.num_programs(0) - 1)
    def _():
        row = lax.broadcasted_iota(jnp.int32, (HEAD_ROWS, head_dim), 0)
        for place in range(pairs):
            mixed = acc_s[place] / sum_s[place][:, :1]
            own = jnp.where(
                row < Q_HEADS // KV_HEADS, mixed[:, :head_dim], mixed[:, head_dim:]
            )
            o_ref[order_ref[place]] = own.astype(o_ref.dtype)


def request_plan(parents, lengths, context, key_block):
    steps_count, beams = parents.shape
    beam_range = jnp.arange(beams, dtype=jnp.int32)
    pairs = steps_count * beams

    def follow(before, step):
        hit = parents[step][:, None] == beam_range[None, :]
        return jnp.sum(jnp.where(hit, before[None, :], 0), axis=1)

    root = beam_range
    roots = []
    live_from = []
    seen = []
    for step in range(steps_count):
        root = follow(root, step)
        roots.append(root)
        live_from = [follow(before, step) for before in live_from] + [beam_range]
        blocks = [
            (before[:, None] == beam_range[None, :]).astype(jnp.float32) for before in live_from
        ]
        blocks += [jnp.zeros((beams, beams), jnp.float32)] * (steps_count - step - 1)
        seen.append(jnp.concatenate(blocks, axis=1))
    seen = jnp.concatenate(seen, axis=0)
    flat = jnp.concatenate(roots)
    index = jnp.arange(pairs, dtype=jnp.int32)
    before = (flat[None, :] < flat[:, None]) | (
        (flat[None, :] == flat[:, None]) & (index[None, :] < index[:, None])
    )
    rank = jnp.sum(before.astype(jnp.int32), axis=1)
    hit = rank[None, :] == index[:, None]
    order = jnp.sum(jnp.where(hit, index[None, :], 0), axis=1)
    seen = jnp.sum(jnp.where(hit[:, :, None], seen[None], 0.0), axis=1)
    seen = jnp.repeat(seen, HEAD_ROWS, axis=0)
    begin = jnp.sum((flat[None, :] < beam_range[:, None]).astype(jnp.int32), axis=1)
    count = jnp.sum((flat[None, :] == beam_range[:, None]).astype(jnp.int32), axis=1)
    per_beam = context // key_block
    items = jnp.arange(beams * per_beam, dtype=jnp.int32)
    first = jnp.arange(per_beam, dtype=jnp.int32) * key_block
    valid = ((count > 0)[:, None] & (first[None, :] < lengths[:, None])).reshape(-1)
    total = jnp.sum(valid.astype(jnp.int32))
    ahead = jnp.sum(
        (valid[None, :] & (items[None, :] < items[:, None])).astype(jnp.int32), axis=1
    )
    wanted = jnp.minimum(items, total - 1)
    chosen = valid[None, :] & (ahead[None, :] == wanted[:, None])
    chosen = jnp.sum(jnp.where(chosen, items[None, :], 0), axis=1)
    return (
        order,
        begin,
        count,
        lengths,
        chosen // per_beam,
        chosen % per_beam,
        total.reshape(1),
        seen,
    )


def beam_attention(queries, new_keys, new_values, cache_keys, cache_values, plan, key_block):
    pairs, heads, head_dim = queries.shape
    beams, context, width = cache_keys.shape
    group = heads // KV_HEADS
    scalars, seen = plan[:-1], plan[-1]
    zero = jnp.zeros((pairs, group, head_dim), queries.dtype)
    spread = jnp.concatenate(
        [
            jnp.concatenate([queries[:, :group], zero], axis=2),
            jnp.concatenate([zero, queries[:, group:]], axis=2),
            jnp.zeros((pairs, HEAD_ROWS - heads, width), queries.dtype),
        ],
        axis=1,
    )

    def whole(shape):
        return pl.BlockSpec(shape, lambda i, *refs: (0,) * len(shape))

    def cached(i, order, begin, count, limit, beam, block, total):
        return (beam[i], block[i], 0)

    items = scalars[4].shape[0]
    return pl.pallas_call(
        functools.partial(attention_kernel, pairs),
        out_shape=jax.ShapeDtypeStruct((pairs, HEAD_ROWS, head_dim), jnp.bfloat16),
        grid_spec=pltpu.PrefetchScalarGridSpec(
            num_scalar_prefetch=7,
            grid=(items,),
            in_specs=[
                whole(spread.shape),
                whole(new_keys.shape),
                whole(new_values.shape),
                whole(seen.shape),
                pl.BlockSpec((None, key_block, width), cached),
                pl.BlockSpec((None, key_block, width), cached),
            ],
            out_specs=whole((pairs, HEAD_ROWS, head_dim)),
            scratch_shapes=[
                pltpu.VMEM((pairs + CHUNK, HEAD_ROWS, width), jnp.bfloat16),
                pltpu.VMEM((pairs + CHUNK, HEAD_ROWS, 128), jnp.float32),
                pltpu.VMEM((pairs + CHUNK, HEAD_ROWS, 128), jnp.float32),
                pltpu.VMEM((pairs + CHUNK, HEAD_ROWS, width), jnp.float32),
            ],
        ),
        compiler_params=pltpu.CompilerParams(vmem_limit_bytes=56 * 1024 * 1024),
        name="beam_attention",
    )(*scalars, spread, new_keys, new_values, seen, cache_keys, cache_values)[:, :heads]


def start_send(source, target, send_sem, recv_sem, peer):
    copy = pltpu.make_async_remote_copy(
        src_ref=source,
        dst_ref=target,
        send_sem=send_sem,
        recv_sem=recv_sem,
        device_id={"tp": peer},
        device_id_type=MESH,
    )
    copy.start()
    return copy


def layer_kernel(
    req_count,
    tp_count,
    pick_ref,
    att_ref,
    x_ref,
    ow_hbm,
    gw_hbm,
    uw_hbm,
    dw_hbm,
    o_ref,
    first,
    second,
    part_a,
    part_b,
    pair_a,
    pair_b,
    joined_a,
    joined_b,
    landed_a,
    landed_b,
    mixed,
    ow,
    gw,
    uw,
    dw,
    sends,
    recvs,
    load_sems,
):
    req_me = lax.axis_index("req")
    tp_me = lax.axis_index("tp")
    chips = tp_count // 2
    chip = tp_me // 2
    core = lax.rem(tp_me, 2)
    other = 1 - core
    partner = chip * 2 + other
    rows, width = x_ref.shape
    weights = ((ow_hbm, ow), (gw_hbm, gw), (uw_hbm, uw), (dw_hbm, dw))
    loads = [
        pltpu.make_async_copy(far, near, load_sems.at[index])
        for index, (far, near) in enumerate(weights)
    ]
    for load in loads:
        load.start()
    greet((("tp", tp_count), ("req", req_count)))
    copies = start_exchange(
        "tp",
        tp_count,
        lambda peer: att_ref.at[peer],
        lambda me: first.at[me],
        sends.at[0],
        recvs.at[0],
    )
    first[tp_me] = att_ref[tp_me]
    wait_all(copies)
    group = pl.ds(req_me * tp_count, tp_count)
    copies = start_exchange(
        "req", req_count, lambda peer: first, lambda me: second.at[group], sends.at[1], recvs.at[1]
    )
    second[group] = first[...]
    wait_all(copies)
    loads[0].wait()
    behind = [lax.rem(chip - hop + chips, chips) for hop in range(chips)]
    ahead = [lax.rem(chip + hop, chips) for hop in range(chips)]
    far_first = list(range(1, chips)) + [0]

    pairs = {}
    for hop in far_first:
        picked = jnp.concatenate(
            [second[pick_ref[behind[hop] * 2 + side]] for side in range(2)], axis=0
        )
        product = jnp.dot(picked, ow[...], preferred_element_type=jnp.float32)
        part_a[hop] = product.astype(jnp.bfloat16).reshape(2, rows, width)
        pairs[hop] = start_send(
            part_a.at[hop, other], pair_a.at[hop], sends.at[2, hop], recvs.at[2, hop], partner
        )
    outs = []
    for hop in far_first:
        pairs[hop].wait()
        both = part_a[hop, core].astype(jnp.float32) + pair_a[hop].astype(jnp.float32)
        if hop:
            joined_a[hop] = both.astype(jnp.bfloat16)
            outs.append(
                start_send(
                    joined_a.at[hop],
                    landed_a.at[hop],
                    sends.at[3, hop],
                    recvs.at[3, hop],
                    behind[hop] * 2 + core,
                )
            )
    wait_all(outs)
    middle = x_ref[...].astype(jnp.float32) + both
    for hop in range(1, chips):
        middle = middle + landed_a[hop].astype(jnp.float32)
    factor = lax.rsqrt(jnp.mean(middle * middle, axis=-1, keepdims=True) + norm_eps)
    mixed[0, core] = (middle * factor).astype(jnp.bfloat16)
    direct = {}
    for hop in range(1, chips):
        direct[hop] = start_send(
            mixed.at[0, core],
            mixed.at[hop, core],
            sends.at[4, hop],
            recvs.at[4, hop],
            ahead[hop] * 2 + core,
        )
    passed = [
        start_send(
            mixed.at[0, core], mixed.at[0, core], sends.at[5, 0], recvs.at[5, 0], partner
        )
    ]

    def take(hop):
        direct[hop].wait()
        passed.append(
            start_send(
                mixed.at[hop, core],
                mixed.at[hop, core],
                sends.at[5, hop],
                recvs.at[5, hop],
                partner,
            )
        )

    half = chips // 2
    for hop in range(1, half):
        take(hop)
    for load in loads[1:]:
        load.wait()
    contract = (((1,), (1,)), ((), ()))
    pairs = {}

    def feed(start):
        block = mixed[start : start + half].reshape(half * 2 * rows, width)
        gate = lax.dot_general(block, gw[...], contract, preferred_element_type=jnp.float32)
        upward = lax.dot_general(block, uw[...], contract, preferred_element_type=jnp.float32)
        hidden = (gate * jax.nn.sigmoid(gate) * upward).astype(jnp.bfloat16)
        product = jnp.dot(hidden, dw[...], preferred_element_type=jnp.float32)
        part_b[start : start + half] = product.astype(jnp.bfloat16).reshape(half, 2, rows, width)
        for hop in range(start, start + half):
            pairs[hop] = start_send(
                part_b.at[hop, other], pair_b.at[hop], sends.at[6, hop], recvs.at[6, hop], partner
            )

    outs = []

    def forward(hop):
        pairs[hop].wait()
        both = part_b[hop, core].astype(jnp.float32) + pair_b[hop].astype(jnp.float32)
        joined_b[hop] = both.astype(jnp.bfloat16)
        outs.append(
            start_send(
                joined_b.at[hop],
                landed_b.at[hop],
                sends.at[7, hop],
                recvs.at[7, hop],
                behind[hop] * 2 + core,
            )
        )

    wait_all(passed[:half])
    feed(0)
    for hop in range(half, chips):
        take(hop)
    for hop in range(1, half):
        forward(hop)
    wait_all(passed[half:])
    feed(half)
    for hop in range(half, chips):
        forward(hop)
    pairs[0].wait()
    result = middle + part_b[0, core].astype(jnp.float32) + pair_b[0].astype(jnp.float32)
    wait_all(outs)
    for hop in range(1, chips):
        result = result + landed_b[hop].astype(jnp.float32)
    o_ref[...] = result.astype(o_ref.dtype)


def layer(attention, pick, x, out_weight, gate_weight, up_weight, down_weight, req_count, tp_count):
    rows, width = x.shape
    piece = attention.shape[2]
    chips = tp_count // 2
    most = max(req_count, tp_count)
    vmem = pl.BlockSpec(memory_space=pltpu.VMEM)
    far = pl.BlockSpec(memory_space=pl.ANY)
    gate_weight, up_weight = gate_weight.T, up_weight.T
    weights = (out_weight, gate_weight, up_weight, down_weight)
    whole = pltpu.VMEM((chips, 2, rows, width), jnp.bfloat16)
    single = pltpu.VMEM((chips, rows, width), jnp.bfloat16)
    return pl.pallas_call(
        functools.partial(layer_kernel, req_count, tp_count),
        out_shape=jax.ShapeDtypeStruct((rows, width), jnp.bfloat16),
        in_specs=[pl.BlockSpec(memory_space=pltpu.SMEM), vmem, vmem, far, far, far, far],
        out_specs=vmem,
        scratch_shapes=[
            pltpu.VMEM((tp_count, rows, piece), jnp.bfloat16),
            pltpu.VMEM((req_count * tp_count, rows, piece), jnp.bfloat16),
            whole,
            whole,
            single,
            single,
            single,
            single,
            single,
            single,
            whole,
        ]
        + [pltpu.VMEM(weight.shape, jnp.bfloat16) for weight in weights]
        + [
            pltpu.SemaphoreType.DMA((8, most)),
            pltpu.SemaphoreType.DMA((8, most)),
            pltpu.SemaphoreType.DMA((4,)),
        ],
        compiler_params=pltpu.CompilerParams(
            collective_id=1, has_side_effects=True, vmem_limit_bytes=56 * 1024 * 1024
        ),
        name="layer",
    )(pick, attention, x, *weights)


def per_device_whole(
    step_inputs,
    qkv_weight,
    qkv_bias,
    out_weight,
    gate_weight,
    up_weight,
    down_weight,
    cache_keys,
    cache_values,
    lengths,
    parents,
    slot_request,
):
    steps_count, beams, width = step_inputs.shape
    requests = slot_request.shape[0]
    req_count = lax.axis_size("req")
    tp_count = lax.axis_size("tp")
    context, kv_width = cache_keys.shape[1:]
    head_dim = kv_width // KV_HEADS
    attn_width = Q_HEADS * head_dim
    req_index = lax.axis_index("req")
    flat_index = req_index * tp_count + lax.axis_index("tp")
    rows = steps_count * beams
    key_block = min(KEY_BLOCK, context)
    request_range = jnp.arange(requests, dtype=jnp.int32)
    inverse = jnp.sum(
        jnp.where(slot_request[None, :] == request_range[:, None], request_range[None, :], 0),
        axis=1,
    )
    group_base = req_index * tp_count
    pick_slots = lax.dynamic_slice_in_dim(inverse, group_base, tp_count)
    pick_requests = lax.dynamic_slice_in_dim(slot_request, group_base, tp_count)

    mine = slot_request[flat_index]
    my_parents = lax.dynamic_index_in_dim(parents, mine, 1, keepdims=False)
    my_lengths = lax.dynamic_index_in_dim(lengths, mine, 0, keepdims=False)
    beam_range = jnp.arange(beams, dtype=jnp.int32)
    positions = []
    root_length = my_lengths
    for step in range(steps_count):
        hit = my_parents[step][:, None] == beam_range[None, :]
        root_length = jnp.sum(jnp.where(hit, root_length[None, :], 0), axis=1)
        positions.append(root_length + step)
    positions = jnp.concatenate(positions)

    inputs = step_inputs.reshape(rows, width)
    qkv = (
        jnp.dot(rms_normed(inputs), qkv_weight, preferred_element_type=jnp.float32) + qkv_bias
    ).astype(jnp.bfloat16)
    turned_width = attn_width + kv_width
    turned = rotate(qkv[:, :turned_width].reshape(rows, -1, head_dim), positions)
    packed = jnp.concatenate([turned.reshape(rows, turned_width), qkv[:, turned_width:]], axis=1)
    routed = route(packed, pick_slots, req_count, tp_count)
    routed = routed.transpose(1, 0, 2).reshape(rows, -1)

    own_parents = lax.dynamic_index_in_dim(parents, flat_index, 1, keepdims=False)
    own_lengths = lax.dynamic_index_in_dim(lengths, flat_index, 0, keepdims=False)
    plan = request_plan(own_parents, own_lengths, context, key_block)
    attention = beam_attention(
        routed[:, :attn_width].reshape(rows, Q_HEADS, head_dim),
        routed[:, attn_width:turned_width],
        routed[:, turned_width:],
        cache_keys,
        cache_values,
        plan,
        key_block,
    )
    pieces = attention.reshape(rows, tp_count, attn_width // tp_count).transpose(1, 0, 2)
    result = layer(
        pieces,
        pick_requests,
        inputs,
        out_weight,
        gate_weight,
        up_weight,
        down_weight,
        req_count,
        tp_count,
    )
    return result.reshape(steps_count, beams, width)


def per_device(*arrays):
    step_inputs, qkv_weight, cache_keys, parents = arrays[0], arrays[1], arrays[7], arrays[10]
    beams = parents.shape[2]
    tp_count = lax.axis_size("tp")
    whole = (
        step_inputs.shape[1] == beams
        and cache_keys.shape[0] == beams
        and tp_count % 4 == 0
        and qkv_weight.shape[1] % (128 * tp_count) == 0
        and cache_keys.shape[1] % min(KEY_BLOCK, cache_keys.shape[1]) == 0
    )
    return (per_device_whole if whole else per_device_split)(*arrays)


def solution(mesh):
    in_specs = (
        P(None, ("req", "tp"), None),
        P(),
        P(),
        P("tp", None),
        P(None, "tp"),
        P(None, "tp"),
        P("tp", None),
        P(("req", "tp"), None, None),
        P(("req", "tp"), None, None),
        P(),
        P(),
        P(),
    )
    out_specs = P(None, ("req", "tp"), None)
    return jax.shard_map(
        per_device, mesh=mesh, in_specs=in_specs, out_specs=out_specs, check_vma=False
    )
```

profile of v0, /device:TPU:0, one launch (start us, length us, event | category | flops | bytes accessed | tf_op | source)
XLA Modules:
  0.0 129.0 jit_solution(4863358527029293564)
XLA Ops:
  0.0 1.2 dynamic_slice.27
  3.2 1.3 %dynamic_slice.23.pick_ref = s32[8]{0:T(128)} dynamic-slice(s32[32]{0:T(128)} %param.23, s32[]{:T(128)S(6)} %select_n.85), dynamic_slice_sizes={8} | dynamic-slice | bytes 68 | tf_op jit(solution)/shard_map/dynamic_slice | solution.py:803
  4.5 0.8 select_reduce_fusion.1
  5.2 0.1 dynamic_slice.26.pick_ref
  5.3 0.1 pad.17.clone
  5.4 1.0 dynamic-slice_reduce_fusion.8
  6.4 0.0 copy-start
  6.4 1.1 dynamic-slice_reduce_fusion
  7.5 0.2 select_reduce_fusion.13
  7.7 0.2 select_reduce_fusion.12
  7.9 0.2 select_reduce_fusion.11
  8.1 0.2 select_reduce_fusion.17
  8.3 0.2 select_reduce_fusion.9
  8.5 0.2 select_reduce_fusion.8
  8.7 0.3 select_reduce_fusion.6
  8.9 0.1 pad_add_fusion
  9.0 0.2 convert_reduce_fusion
  9.2 0.7 select_reduce_fusion.2.order_ref
  9.9 0.1 add_convert_fusion.1
  9.9 0.6 convert_reduce_fusion.3
  10.6 0.0 copy-start.1
  10.6 0.8 convert_reduce_fusion.2
  12.0 0.1 and.49
  12.1 0.1 convert_reduce_fusion.1
  12.2 0.2 select_reduce_fusion.3
  12.4 0.6 and_select_fusion
  13.0 1.0 multiply_reduce_fusion
  14.0 0.1 rsqrt.12
  14.1 0.1 fusion.16
  14.2 0.1 fusion.18
  14.3 0.1 fusion.17
  14.3 0.1 fusion.14
  14.4 0.1 fusion.12
  14.5 0.1 fusion.8
  14.6 0.2 select_reduce_fusion
  14.8 0.1 multiply_cosine_fusion
  14.9 4.0 %fusion = bf16[32,2048]{1,0:T(8,128)(2,1)S(1)} fusion(bf16[1536,2048]{1,0:T(8,128)(2,1)} %param.13, f32[2048]{0:T(1024)} %param.14, f32[32]{0:T(128)S(1)} %rsqrt.12, bf16[4,8,1536]{2,1,0:T(8,128)(2,1)} %param.12), kind=kOutput, calls=%fused_computation.1 | convolution fusion | flops 201605120 | bytes 6529152 | tf_op jit(solution)/shard_map/dot_general | solution.py:819
  19.1 0.2 subtract_convert_fusion
  19.3 0.1 pad_maximum_fusion
  19.4 22.7 %route.1 = bf16[8,32,256]{2,1,0:T(8,128)(2,1)S(1)} custom-call(s32[8]{0:T(128)S(1)} %dynamic_slice.26.pick_ref, bf16[32,2048]{1,0:T(8,128)(2,1)S(1)} %pad_maximum_fusion.1.x_ref), custom_call_target="tpu_custom_call" | custom-call | tf_op jit(solution)/shard_map/route/pallas_call | solution.py:305
  42.1 0.6 fusion.20
  42.8 0.1 reshape.227
  42.9 0.8 fusion.5.q_ref
  43.7 0.7 broadcast_in_dim.237
  44.4 0.0 copy-done
  44.4 0.0 copy-done.1
  44.4 20.7 %beam_attention.1 = bf16[32,16,128]{2,1,0:T(8,128)(2,1)} custom-call(s32[32]{0:T(128)} %select_reduce_fusion.2.order_ref, s32[8]{0:T(128)} %get-tuple-element.25.begin_ref, s32[8]{0:T(128)} %copy-done.1, s32[8]{0:T(128)} %copy-done, s32[16]{0:T(128)} %get-tuple-element.37.beam_ref, s32[16]{0:T(128)} %get-tuple-element.36.block_ref, s32[1]{0:T(128)} %bitcast.total_ref, ...), custom_call_target="tpu_custom_call" | custom-call | tf_op jit(solution)/shard_map/beam_attention/pallas_call | solution.py:510
  65.1 1.1 reshape.229
  66.1 0.7 copy.22
  66.8 60.6 %layer.1 = bf16[32,1536]{1,0:T(8,128)(2,1)} custom-call(s32[8]{0:T(128)} %dynamic_slice.23.pick_ref, bf16[8,32,192]{2,1,0:T(8,128)(2,1)} %bitcast.29, bf16[32,1536]{1,0:T(8,128)(2,1)} %bitcast.27, bf16[192,1536]{1,0:T(8,128)(2,1)} %ow_hbm.1, bf16[1120,1536]{1,0:T(8,128)(2,1)} %bitcast.24, bf16[1120,1536]{1,0:T(8,128)(2,1)} %bitcast.25, bf16[1120,1536]{1,0:T(8,128)(2,1)} %dw_hbm.1), custom_call_target="tpu_custom_call" | custom-call | tf_op jit(solution)/shard_map/layer/pallas_call | solution.py:740
  127.4 1.5 %copy.25 = bf16[4,8,1536]{2,1,0:T(8,128)(2,1)} copy(bf16[4,8,1536]{2,1,0:T(8,128)(2,1)} %bitcast.34) | data formatting | bytes 196608
  (19 shorter events, 0.2 us)
Async XLA Ops:
  6.4 38.0 %copy-start = (s32[8]{0:T(128)}, s32[8]{0:T(128)S(1)}, u32[]{:S(2)}) copy-start(s32[8]{0:T(128)S(1)} %get-tuple-element.14.limit_ref) | copy-start | bytes 100
  10.6 33.8 %copy-start.1 = (s32[8]{0:T(128)}, s32[8]{0:T(128)S(1)}, u32[]{:S(2)}) copy-start(s32[8]{0:T(128)S(1)} %get-tuple-element.24.count_ref) | copy-start | bytes 100
where the time goes:
time: 129 us
  Pallas kernels  104 us (81%)
  local copies, waits for them, and re-layouts  9.77 us (8%)
  other arithmetic  8.41 us (7%)
  matrix products  4.03 us (3%)
  between operations  2.79 us (2%)
    pallas_call x1, Pallas kernels, layer(): pl.pallas_call(functools.partial(layer_kernel, req_count, tp_count), out_...  60.6 us
    pallas_call x1, Pallas kernels, route(): pl.pallas_call(functools.partial(route_kernel, req_count, tp_count), out_...  22.7 us
    pallas_call x1, Pallas kernels, beam_attention(): pl.pallas_call(functools.partial(attention_kernel, pairs), out_shape=jax....  20.7 us
    dot_general x1, matrix products, per_device_whole(): jnp.dot(rms_normed(inputs), qkv_weight, preferred_element_type=jnp.float32)  4.03 us

commit v1 on v0

--- a/solution.py
+++ b/solution.py
@@ -222,7 +222,8 @@
     return jnp.stack(results)
 
 MESH = pl.DeviceIdType.MESH
-CHUNK = 4
+SMALL = 4
+CHUNK = 8
 KEY_BLOCK = 2048
 HEAD_ROWS = 16
 
@@ -385,18 +386,16 @@
         begin = begin_ref[beam]
         end = begin + count_ref[beam]
         left = limit_ref[beam] - block_ref[item] * key_block
-        rows = CHUNK * HEAD_ROWS
-
-        def one_chunk(index, carry):
-            base = begin + index * CHUNK
-            span = pl.ds(base, CHUNK)
+        def one_chunk(base, size, keys):
+            rows = size * HEAD_ROWS
+            span = pl.ds(base, size)
             scores = scale * lax.dot_general(
                 qs[span].reshape(rows, width),
-                k_ref[...],
+                k_ref[:keys],
                 contract,
                 preferred_element_type=jnp.float32,
             )
-            place = lax.broadcasted_iota(jnp.int32, (rows, key_block), 1)
+            place = lax.broadcasted_iota(jnp.int32, (rows, keys), 1)
             row = lax.broadcasted_iota(jnp.int32, (rows, 1), 0)
             live = place < jnp.where(row < (end - base) * HEAD_ROWS, left, 0)
             scores = jnp.where(live, scores, masked_score)
@@ -407,14 +406,34 @@
             total = sum_s[span].reshape(rows, 128)[:, :1] * fade
             total = total + jnp.sum(weights, axis=1, keepdims=True)
             mixed = acc_s[span].reshape(rows, width) * fade + jnp.dot(
-                weights.astype(jnp.bfloat16), v_ref[...], preferred_element_type=jnp.float32
+                weights.astype(jnp.bfloat16), v_ref[:keys], preferred_element_type=jnp.float32
             )
-            top_s[span] = jnp.broadcast_to(top, (rows, 128)).reshape(CHUNK, HEAD_ROWS, 128)
-            sum_s[span] = jnp.broadcast_to(total, (rows, 128)).reshape(CHUNK, HEAD_ROWS, 128)
-            acc_s[span] = mixed.reshape(CHUNK, HEAD_ROWS, width)
-            return carry
-
-        lax.fori_loop(0, lax.div(end - begin + CHUNK - 1, CHUNK), one_chunk, 0)
+            top_s[span] = jnp.broadcast_to(top, (rows, 128)).reshape(size, HEAD_ROWS, 128)
+            sum_s[span] = jnp.broadcast_to(total, (rows, 128)).reshape(size, HEAD_ROWS, 128)
+            acc_s[span] = mixed.reshape(size, HEAD_ROWS, width)
+
+        large = lax.div(end - begin + CHUNK - SMALL - 1, CHUNK)
+
+        rest = begin + large * CHUNK
+
+        def all_chunks(keys):
+            def large_chunk(index, carry):
+                one_chunk(begin + index * CHUNK, CHUNK, keys)
+                return carry
+
+            lax.fori_loop(0, large, large_chunk, 0)
+
+            @pl.when(rest < end)
+            def _():
+                one_chunk(rest, SMALL, keys)
+
+        @pl.when(left > key_block // 2)
+        def _():
+            all_chunks(key_block)
+
+        @pl.when(left <= key_block // 2)
+        def _():
+            all_chunks(key_block // 2)
 
     @pl.when(item == pl.num_programs(0) - 1)
     def _():

time: 129 us -> 124 us (0.961)
  Pallas kernels: 104 us -> 98.6 us
    pallas_call x1, Pallas kernels: 60.6 us -> 56 us  [layer(): pl.pallas_call(functools.partial(layer_kernel, req_count, tp_count), out_...]
where the time goes in v1:
time: 124 us
  Pallas kernels  98.6 us (80%)
  local copies, waits for them, and re-layouts  9.77 us (8%)
  other arithmetic  8.41 us (7%)
  matrix products  4.03 us (3%)
  between operations  2.79 us (2%)
    pallas_call x1, Pallas kernels, layer(): pl.pallas_call(functools.partial(layer_kernel, req_count, tp_count), out_...  56 us
    pallas_call x1, Pallas kernels, route(): pl.pallas_call(functools.partial(route_kernel, req_count, tp_count), out_...  22.7 us
    pallas_call x1, Pallas kernels, beam_attention(): pl.pallas_call(functools.partial(attention_kernel, pairs), out_shape=jax....  19.8 us
    dot_general x1, matrix products, per_device_whole(): jnp.dot(rms_normed(inputs), qkv_weight, preferred_element_type=jnp.float32)  4.03 us

profile of v1, /device:TPU:0, one launch (start us, length us, event | category | flops | bytes accessed | tf_op | source)
XLA Modules:
  0.0 123.5 jit_solution(3792533044648946282)
XLA Ops:
  0.0 1.2 %dynamic_slice.27 = s32[1]{0:T(128)} dynamic-slice(s32[32]{0:T(128)} %param.23, s32[]{:T(128)S(6)} %select_n.86), dynamic_slice_sizes={1} | dynamic-slice | bytes 12 | tf_op jit(solution)/shard_map/dynamic_slice | solution.py:824
  3.2 1.3 %dynamic_slice.23.pick_ref = s32[8]{0:T(128)} dynamic-slice(s32[32]{0:T(128)} %param.23, s32[]{:T(128)S(6)} %select_n.85), dynamic_slice_sizes={8} | dynamic-slice | bytes 68 | tf_op jit(solution)/shard_map/dynamic_slice | solution.py:822
  4.5 0.8 select_reduce_fusion.1
  5.2 0.1 dynamic_slice.26.pick_ref
  5.3 0.1 pad.17.clone
  5.4 1.0 dynamic-slice_reduce_fusion.8
  6.4 0.0 copy-start
  6.4 1.1 dynamic-slice_reduce_fusion
  7.5 0.2 select_reduce_fusion.13
  7.7 0.2 select_reduce_fusion.12
  7.9 0.2 select_reduce_fusion.11
  8.1 0.2 select_reduce_fusion.17
  8.3 0.2 select_reduce_fusion.9
  8.5 0.2 select_reduce_fusion.8
  8.7 0.3 select_reduce_fusion.6
  8.9 0.1 pad_add_fusion
  9.0 0.2 convert_reduce_fusion
  9.2 0.7 select_reduce_fusion.2.order_ref
  9.9 0.1 add_convert_fusion.1
  9.9 0.6 convert_reduce_fusion.3
  10.6 0.0 copy-start.1
  10.6 0.8 convert_reduce_fusion.2
  12.0 0.1 and.49
  12.1 0.1 convert_reduce_fusion.1
  12.2 0.2 select_reduce_fusion.3
  12.4 0.6 and_select_fusion
  13.0 1.0 multiply_reduce_fusion
  14.0 0.1 rsqrt.12
  14.1 0.1 fusion.16
  14.2 0.1 fusion.18
  14.3 0.1 fusion.17
  14.3 0.1 fusion.14
  14.4 0.1 fusion.12
  14.5 0.1 fusion.8
  14.6 0.2 select_reduce_fusion
  14.8 0.1 multiply_cosine_fusion
  14.9 4.0 %fusion = bf16[32,2048]{1,0:T(8,128)(2,1)S(1)} fusion(bf16[1536,2048]{1,0:T(8,128)(2,1)} %param.13, f32[2048]{0:T(1024)} %param.14, f32[32]{0:T(128)S(1)} %rsqrt.12, bf16[4,8,1536]{2,1,0:T(8,128)(2,1)} %param.12), kind=kOutput, calls=%fused_computation.1 | convolution fusion | flops 201605120 | bytes 6529152 | tf_op jit(solution)/shard_map/dot_general | solution.py:838
  19.1 0.2 subtract_convert_fusion
  19.3 0.1 pad_maximum_fusion
  19.4 22.7 %route.1 = bf16[8,32,256]{2,1,0:T(8,128)(2,1)S(1)} custom-call(s32[8]{0:T(128)S(1)} %dynamic_slice.26.pick_ref, bf16[32,2048]{1,0:T(8,128)(2,1)S(1)} %pad_maximum_fusion.1.x_ref), custom_call_target="tpu_custom_call" | custom-call | tf_op jit(solution)/shard_map/route/pallas_call | solution.py:306
  42.1 0.6 fusion.20
  42.8 0.1 reshape.227
  42.9 0.8 fusion.5.q_ref
  43.7 0.7 broadcast_in_dim.237
  44.4 0.0 copy-done
  44.4 0.0 copy-done.1
  44.4 19.8 %beam_attention.1 = bf16[32,16,128]{2,1,0:T(8,128)(2,1)} custom-call(s32[32]{0:T(128)} %select_reduce_fusion.2.order_ref, s32[8]{0:T(128)} %get-tuple-element.25.begin_ref, s32[8]{0:T(128)} %copy-done.1, s32[8]{0:T(128)} %copy-done, s32[16]{0:T(128)} %get-tuple-element.37.beam_ref, s32[16]{0:T(128)} %get-tuple-element.36.block_ref, s32[1]{0:T(128)} %bitcast.total_ref, ...), custom_call_target="tpu_custom_call" | custom-call | tf_op jit(solution)/shard_map/beam_attention/pallas_call | solution.py:529
  64.3 1.1 reshape.229
  65.3 0.7 copy.22
  66.0 56.0 %layer.1 = bf16[32,1536]{1,0:T(8,128)(2,1)} custom-call(s32[8]{0:T(128)} %dynamic_slice.23.pick_ref, bf16[8,32,192]{2,1,0:T(8,128)(2,1)} %bitcast.29, bf16[32,1536]{1,0:T(8,128)(2,1)} %bitcast.27, bf16[192,1536]{1,0:T(8,128)(2,1)} %ow_hbm.1, bf16[1120,1536]{1,0:T(8,128)(2,1)} %bitcast.24, bf16[1120,1536]{1,0:T(8,128)(2,1)} %bitcast.25, bf16[1120,1536]{1,0:T(8,128)(2,1)} %dw_hbm.1), custom_call_target="tpu_custom_call" | custom-call | tf_op jit(solution)/shard_map/layer/pallas_call | solution.py:759
  122.0 1.5 %copy.25 = bf16[4,8,1536]{2,1,0:T(8,128)(2,1)} copy(bf16[4,8,1536]{2,1,0:T(8,128)(2,1)} %bitcast.34) | data formatting | bytes 196608
  (19 shorter events, 0.2 us)
Async XLA Ops:
  6.4 38.0 %copy-start = (s32[8]{0:T(128)}, s32[8]{0:T(128)S(1)}, u32[]{:S(2)}) copy-start(s32[8]{0:T(128)S(1)} %get-tuple-element.14.limit_ref) | copy-start | bytes 100
  10.6 33.8 %copy-start.1 = (s32[8]{0:T(128)}, s32[8]{0:T(128)S(1)}, u32[]{:S(2)}) copy-start(s32[8]{0:T(128)S(1)} %get-tuple-element.24.count_ref) | copy-start | bytes 100
